TPU v7x, 512 devices: a whole 4x4x16 slice. The times are simulated.
512 devices in a mesh: row: 32 (over z, core), col: 16 (over x, y).
Axes of the slice: x: 4, y: 4, z: 16, core: 2. Of those that a mesh axis runs over, the one named last changes fastest.
Arguments:
- rhs: bfloat16 [3, 32, 64, 256], P(None, 'row'), may hold values from -6 to 6
- dinv: bfloat16 [3, 32, 256, 256], P(None, 'row'), as said below
- tiles: bfloat16 [2, 32, 32, 256, 256], P(None, 'row', 'col'), may hold values from -0.046875 to 0.046875
- pattern: int32 [2, 2, 32, 32], P(None, None, 'row', 'col'), may hold values from 0 to 31, as said below
Outputs:
- solution: float32 [3, 32, 64, 256], P(None, 'row')
Inputs may be any that keep to these rules, and one draw needn't show every extreme that they name: pattern[0, l, p, t] = p; pattern[1, l, p, t] = j has (j) modulo the size of col equal to t // 2; positions may repeat, and repeated tiles add. `dinv`: lower triangular with a positive diagonal.
All inputs are finite; a program needn't handle non-finite values.
Results may differ from a plain program's by a relative error of at most 0.0055.
Values may be sent and summed in bfloat16 or wider, within the bound.
A program may use at most 64 MiB of HBM per device.

v0:
```python
import jax
import jax.numpy as jnp
from jax import lax
from jax.sharding import PartitionSpec as P


def broadcast(block, axis, holder):
    block = jnp.where(lax.axis_index(axis) == holder, block, jnp.zeros_like(block))
    return lax.psum(block, axis)


def collect(rounded, mine_col, col_count, repeat):
    pieces = []
    for group in range(repeat):
        pieces.append(broadcast(rounded, "row", mine_col + col_count * group))
    return jnp.concatenate(pieces, 0)


def per_device(rhs, dinv, tiles, pattern):
    blocks = rhs.shape[1]
    levels_all = rhs.shape[0]
    col_count = lax.axis_size("col")
    row_count = lax.axis_size("row")
    repeat = row_count // col_count
    mine_row = lax.axis_index("row")
    mine_col = lax.axis_index("col")
    targets = pattern[0, :, 0, :] % blocks
    raw_cols = pattern[1, :, 0, :]
    sources = raw_cols // blocks // col_count * blocks + raw_cols % blocks
    row_pick = (targets[:, None, :] == jnp.arange(blocks, dtype=jnp.int32)[None, :, None]).astype(
        jnp.float32
    )
    col_pick = (
        sources[:, None, :] == jnp.arange(repeat * blocks, dtype=jnp.int32)[None, :, None]
    ).astype(jnp.float32)
    fronts = [rhs]
    forward_all = [[] for front in fronts]
    rounded_all = [None for front in fronts]
    for level_now in range(levels_all):
        front_index = 0
        front_level = fronts[front_index][level_now]
        current = front_level.astype(jnp.float32)
        if level_now > 0:
            nearby = collect(rounded_all[front_index], mine_col, col_count, repeat)
            source = jnp.take(nearby, sources[level_now - 1], axis=0)
            product = jnp.einsum(
                "sjb,sab->sja", source, tiles[level_now - 1, 0], preferred_element_type=jnp.float32
            )
            partial_value = jnp.sum(
                row_pick[level_now - 1][:, :, None, None] * product[None], axis=1
            )
            total_sum = lax.psum(partial_value, "col")
            current = current - total_sum
        solved = jnp.einsum(
            "rjb,rab->rja",
            current.astype(jnp.bfloat16),
            dinv[level_now],
            preferred_element_type=jnp.float32,
        )
        forward_all[front_index].append(solved)
        rounded_all[front_index] = solved.astype(jnp.bfloat16)
    backward_all = [[None] * levels_all for front in fronts]
    following_all = [None for front in fronts]
    for level_now in range(levels_all - 1, -1, -1):
        front_index = 0
        remainder = forward_all[front_index][level_now]
        if level_now < levels_all - 1:
            source = jnp.take(following_all[front_index], targets[level_now], axis=0)
            product = jnp.einsum(
                "sja,sab->sjb", source, tiles[level_now, 0], preferred_element_type=jnp.float32
            )
            partial_value = jnp.sum(col_pick[level_now][:, :, None, None] * product[None], axis=1)
            column_total = lax.psum(partial_value, "row")
            shaped = column_total.reshape((repeat, blocks) + column_total.shape[1:])
            picked = lax.dynamic_index_in_dim(shaped, mine_row // col_count, 0, keepdims=False)
            arrived = broadcast(picked, "col", mine_row % col_count)
            remainder = remainder - arrived
        solved = jnp.einsum(
            "rjb,rba->rja",
            remainder.astype(jnp.bfloat16),
            dinv[level_now],
            preferred_element_type=jnp.float32,
        )
        backward_all[front_index][level_now] = solved
        following_all[front_index] = solved.astype(jnp.bfloat16)
    front_index = 0
    levels_stack = jnp.stack(backward_all[front_index])
    return levels_stack


def solution(mesh):
    in_specs = (
        P(None, "row", None, None),
        P(None, "row", None, None),
        P(None, "row", "col", None, None),
        P(None, None, "row", "col"),
    )
    out_specs = P(None, "row", None, None)
    return jax.shard_map(
        per_device, mesh=mesh, in_specs=in_specs, out_specs=out_specs, check_vma=False
    )
```

profile of v0, /device:TPU:1, one launch (start us, length us, event | category | flops | bytes accessed | tf_op | source)
XLA Modules:
  0.0 1224.5 jit_solution(12864337464634439809)
XLA Ops:
  6.5 1.1 fusion.18
  7.7 0.7 select_bitcast_fusion.3
  8.4 0.0 all-reduce.11.cloned.1.call-start
  8.4 0.7 slice.51
  9.2 189.5 %all-reduce.25.cloned.1.call-done = (bf16[1,64,256]{2,1,0:T(8,128)(2,1)}, bf16[1,64,256]{2,1,0:T(8,128)(2,1)}) async-done(((bf16[1,64,256]{2,1,0:T(8,128)(2,1)}, bf16[1,64,256]{2,1,0:T(8,128)(2,1)}), (bf16[1,64,256]{2,1,0:T(8,128)(2,1)}, bf16[1,64,256]{2,1,0:T(8,128)(2,1)})) %all-reduce.25.cloned.1.call-update) | async-done | bytes 65552 | tf_op jit(solution)/shard_map/psum | solution.py:9
  198.7 0.8 pad_maximum_fusion.1
  199.4 0.5 gather_fusion
  200.0 0.8 convolution_bitcast_fusion.2
  200.9 104.3 %all-reduce.11.cloned.1.call-done = f32[1,64,256]{2,1,0:T(8,128)} async-done(((f32[1,64,256]{2,1,0:T(8,128)}), f32[1,64,256]{2,1,0:T(8,128)}) %all-reduce.11.cloned.1.call-update) | async-done | bytes 65552 | tf_op jit(solution)/shard_map/psum | solution.py:52
  305.3 1.0 fusion.15
  306.3 0.7 select_bitcast_fusion.1
  307.0 185.6 %all-reduce.23.cloned.1.call-done = (bf16[1,64,256]{2,1,0:T(8,128)(2,1)}, bf16[1,64,256]{2,1,0:T(8,128)(2,1)}) async-done(((bf16[1,64,256]{2,1,0:T(8,128)(2,1)}, bf16[1,64,256]{2,1,0:T(8,128)(2,1)}), (bf16[1,64,256]{2,1,0:T(8,128)(2,1)}, bf16[1,64,256]{2,1,0:T(8,128)(2,1)})) %all-reduce.23.cloned.1.call-update) | async-done | bytes 65552 | tf_op jit(solution)/shard_map/psum | solution.py:9
  492.6 0.8 pad_maximum_fusion.2
  493.4 0.5 gather_fusion.1
  493.9 0.8 convolution_bitcast_fusion.1
  494.9 104.2 %all-reduce.13.cloned.1.call-done = f32[1,64,256]{2,1,0:T(8,128)} async-done(((f32[1,64,256]{2,1,0:T(8,128)}), f32[1,64,256]{2,1,0:T(8,128)}) %all-reduce.13.cloned.1.call-update) | async-done | bytes 65552 | tf_op jit(solution)/shard_map/psum | solution.py:52
  599.0 1.1 fusion.57
  600.2 0.2 fusion.1
  600.4 0.8 multiply_reduce_fusion.1
  601.1 0.0 all-reduce.17.cloned.1.call-start
  601.2 197.0 %all-reduce.15.cloned.1.call-done = f32[2,64,256]{2,1,0:T(8,128)} async-done(((f32[2,64,256]{2,1,0:T(8,128)}), f32[2,64,256]{2,1,0:T(8,128)}) %all-reduce.15.cloned.1.call-update) | async-done | bytes 131088 | tf_op jit(solution)/shard_map/psum | solution.py:73
  798.2 1.5 dynamic-slice_select_fusion.1
  799.7 0.0 all-reduce.19.cloned.1.call-start
  799.7 107.7 %all-reduce.17.cloned.1.call-done = f32[1,64,256]{2,1,0:T(8,128)} async-done(((f32[1,64,256]{2,1,0:T(8,128)}), f32[1,64,256]{2,1,0:T(8,128)}) %all-reduce.17.cloned.1.call-update) | async-done | bytes 65552 | tf_op jit(solution)/shard_map/psum | solution.py:9
  907.4 1.0 fusion.62
  908.4 0.2 fusion.4
  908.5 0.7 multiply_reduce_fusion
  909.4 197.3 %all-reduce.19.cloned.1.call-done = f32[2,64,256]{2,1,0:T(8,128)} async-done(((f32[2,64,256]{2,1,0:T(8,128)}), f32[2,64,256]{2,1,0:T(8,128)}) %all-reduce.19.cloned.1.call-update) | async-done | bytes 131088 | tf_op jit(solution)/shard_map/psum | solution.py:73
  1106.6 1.5 dynamic-slice_select_fusion
  1108.1 107.9 %all-reduce.21.cloned.1.call-done = f32[1,64,256]{2,1,0:T(8,128)} async-done(((f32[1,64,256]{2,1,0:T(8,128)}), f32[1,64,256]{2,1,0:T(8,128)}) %all-reduce.21.cloned.1.call-update) | async-done | bytes 65552 | tf_op jit(solution)/shard_map/psum | solution.py:9
  1216.0 1.0 convolution_bitcast_fusion
  1217.0 0.7 pad_maximum_fusion
  (25 shorter events, 0.4 us)
Async XLA Ops:
  6.5 193.5 %copy-start.1 = (bf16[2,1,2,256,256]{4,3,2,1,0:T(8,128)(2,1)S(1)}, bf16[2,1,2,256,256]{4,3,2,1,0:T(8,128)(2,1)}, u32[]{:S(2)}) copy-start(bf16[2,1,2,256,256]{4,3,2,1,0:T(8,128)(2,1)} %param.10) | copy-start | bytes 1572868
  6.5 192.1 %all-reduce.25.cloned.1.call-start = ((), (), s32[]{:S(2)}) async-start(), calls=%async_computation.7 | async-start | bytes 131072 | tf_op jit(solution)/shard_map/psum | solution.py:9
  8.4 296.9 %copy-start = (bf16[3,1,256,256]{3,2,1,0:T(8,128)(2,1)S(1)}, bf16[3,1,256,256]{3,2,1,0:T(8,128)(2,1)}, u32[]{:S(2)}) copy-start(bf16[3,1,256,256]{3,2,1,0:T(8,128)(2,1)} %param.9) | copy-start | bytes 1179652
  8.4 296.9 %all-reduce.11.cloned.1.call-start = ((), (), s32[]{:S(2)}) async-start(), calls=%async_computation | async-start | bytes 131072 | tf_op jit(solution)/shard_map/psum | solution.py:52
  200.0 105.3 %copy-start.2 = (bf16[3,1,64,256]{3,2,1,0:T(8,128)(2,1)S(1)}, bf16[3,1,64,256]{3,2,1,0:T(8,128)(2,1)}, u32[]{:S(2)}) copy-start(bf16[3,1,64,256]{3,2,1,0:T(8,128)(2,1)} %param.8) | copy-start | bytes 294916
  200.9 291.7 %all-reduce.23.cloned.1.call-start = ((), (), s32[]{:S(2)}) async-start(), calls=%async_computation.6 | async-start | bytes 131072 | tf_op jit(solution)/shard_map/psum | solution.py:9
  307.0 292.1 %all-reduce.13.cloned.1.call-start = ((), (), s32[]{:S(2)}) async-start(), calls=%async_computation.1 | async-start | bytes 131072 | tf_op jit(solution)/shard_map/psum | solution.py:52
  494.8 303.4 %all-reduce.15.cloned.1.call-start = ((), (), s32[]{:S(2)}) async-start(), calls=%async_computation.2 | async-start | bytes 262144 | tf_op jit(solution)/shard_map/psum | solution.py:73
  601.1 306.3 %all-reduce.17.cloned.1.call-start = ((), (), s32[]{:S(2)}) async-start(), calls=%async_computation.3 | async-start | bytes 131072 | tf_op jit(solution)/shard_map/psum | solution.py:9
  799.7 307.0 %all-reduce.19.cloned.1.call-start = ((), (), s32[]{:S(2)}) async-start(), calls=%async_computation.4 | async-start | bytes 262144 | tf_op jit(solution)/shard_map/psum | solution.py:73
  909.3 306.7 %all-reduce.21.cloned.1.call-start = ((), (), s32[]{:S(2)}) async-start(), calls=%async_computation.5 | async-start | bytes 131072 | tf_op jit(solution)/shard_map/psum | solution.py:9
Sparse Core Ops, SparseCore 0:
  9.8 188.8 all-reduce.24
  202.2 103.0 all-reduce.10
  307.7 184.8 all-reduce.22
  496.0 103.0 all-reduce.12
  601.3 196.8 all-reduce.14
  801.5 105.8 all-reduce.16
  909.7 196.8 all-reduce.18
  1110.1 105.8 all-reduce.20
where the time goes:
time: 1230 us; the launch traced here: 1220 us
  waiting for transfers between devices  1190 us (97%)
  between operations  13.6 us (1%)
    psum x4, waiting for transfers between devices, broadcast(): return lax.psum(block, axis)  591 us
    psum x2, waiting for transfers between devices, per_device(): column_total = lax.psum(partial_value, 'row')  394 us
    psum x2, waiting for transfers between devices, per_device(): total_sum = lax.psum(partial_value, 'col')  209 us
  transfers between devices with their start and end apart: 8, of which 8 were waited for; matrix products, arithmetic and copies ran while one was open for 0% of the time, Pallas kernels for 0%

commit v1 on v0

v1 whole, which is shorter than its diff:
```python
import functools

import jax
import jax.numpy as jnp
from jax import lax
from jax.experimental import pallas as pl
from jax.experimental.pallas import tpu as pltpu
from jax.sharding import PartitionSpec as P

MESH = pl.DeviceIdType.MESH
BF16, F32 = jnp.bfloat16, jnp.float32
NT = (((1,), (1,)), ((), ()))
NN = (((1,), (0,)), ((), ()))


def mm(a, b, dims):
    return lax.dot_general(a, b, dims, preferred_element_type=F32)


def kernel(
    dims,
    pat, rhs_hbm, dinv_hbm, tiles_hbm, out,
    rhs, dinv, tiles, load_sem,
    fwd, own, spread, part, red_f, gath, back, red_b,
    self_sem, send_sem, recv_sem,
):
    levels, rows, cols, rep, groups, gr, bs = dims
    nrhs = groups * gr
    slots = tiles.shape[1]
    me_r, me_c = lax.axis_index("row"), lax.axis_index("col")
    side, g_own = lax.rem(me_r, 2), me_c // 2
    home = lax.rem(me_r, cols)
    blk_own = me_r // cols
    is_owner = lax.rem(me_c, 2) == side
    at_home = home == me_c

    loads = [
        pltpu.make_async_copy(rhs_hbm.at[:, g_own], rhs, load_sem.at[0]),
        pltpu.make_async_copy(dinv_hbm, dinv, load_sem.at[1]),
        pltpu.make_async_copy(tiles_hbm, tiles, load_sem.at[2]),
    ]
    for load in loads:
        load.start()

    barrier = pltpu.get_barrier_semaphore()

    def tell(r, c):
        pl.semaphore_signal(barrier, inc=1, device_id=(r, c), device_id_type=MESH)

    def loop(n, body):
        for k in range(n):
            body(k)

    for blk in range(rep):
        def from_owner(k, blk=blk):
            tell(me_c + cols * blk, 2 * lax.rem(g_own + k, groups) + lax.rem(me_c, 2))

        loop(groups, from_owner)
    loop(groups, lambda k: tell(me_r, 2 * lax.rem(g_own + k, groups) + side))

    @pl.when(is_owner)
    def _():
        loop(cols, lambda k: tell(me_r, lax.rem(me_c + k, cols)))
        loop(rows, lambda k: tell(lax.rem(me_r + k, rows), home))
        pl.semaphore_wait(barrier, rows + cols + groups + rep * groups)

    @pl.when(jnp.logical_not(is_owner))
    def _():
        pl.semaphore_wait(barrier, groups + rep * groups)

    def send(src, dst, phase, r, c):
        pltpu.make_async_remote_copy(
            src_ref=src, dst_ref=dst, send_sem=send_sem.at[phase], recv_sem=recv_sem.at[phase],
            device_id=(r, c), device_id_type=MESH,
        ).start()

    def keep(src, dst, phase):
        pltpu.make_async_copy(src, dst, recv_sem.at[phase]).start()

    def arrived(ref, phase):
        pltpu.make_async_copy(ref, ref, recv_sem.at[phase]).wait()

    def sent(ref, phase):
        pltpu.make_async_copy(ref, ref, send_sem.at[phase]).wait()


    phase = 0
    loads[0].wait()
    loads[1].wait()

    for level in range(levels):
        if level == 0:
            @pl.when(is_owner)
            def _():
                fwd[0] = mm(rhs[0], dinv[0], NT)
        else:
            sp, ph_s, ph_r = level - 1, phase, phase + 1
            phase += 2

            @pl.when(is_owner)
            def _(sp=sp, ph_s=ph_s):
                own[sp] = fwd[sp].astype(BF16)
                src, dst = own.at[sp], spread[sp].at[blk_own, g_own]

                def one(k):
                    send(src, dst, ph_s, lax.rem(me_r + k, rows), home)

                for k in range(1, rows):
                    one((k + rows // 2 - 1) % (rows - 1) + 1)

                @pl.when(at_home)
                def _():
                    keep(src, dst, ph_s)

                @pl.when(jnp.logical_not(at_home))
                def _():
                    one(0)

            if level == 1:
                loads[2].wait()
            arrived(spread[sp], ph_s)
            total = None
            for slot in range(slots):
                blk = pat[1, sp, slot] // cols
                source = spread[sp][blk].astype(F32).reshape(nrhs, bs).astype(BF16)
                product = mm(source, tiles[sp, slot], NT)
                total = product if total is None else total + product
            part[sp, 0] = total.astype(BF16).reshape(groups, gr, bs)

            def one(k, sp=sp, ph_r=ph_r):
                g = lax.rem(g_own + k, groups)
                send(part.at[sp, 0, g], red_f.at[sp, me_c], ph_r, me_r, 2 * g + side)

            for k in range(1, groups):
                one(k)

            @pl.when(jnp.logical_not(is_owner))
            def _(one=one):
                one(0)

            @pl.when(is_owner)
            def _(sp=sp, ph_r=ph_r, level=level):
                keep(part.at[sp, 0, g_own], red_f.at[sp, me_c], ph_r)
                arrived(red_f.at[sp], ph_r)
                update = jnp.sum(red_f[sp].astype(F32), axis=0)
                current = rhs[level].astype(F32) - update
                fwd[level] = mm(current.astype(BF16), dinv[level], NT)

    for level in range(levels - 1, -1, -1):
        ph_r = phase
        phase += 1

        @pl.when(is_owner)
        def _(level=level, ph_r=ph_r):
            remainder = fwd[level]
            if level < levels - 1:
                arrived(red_b.at[level], ph_r - 1)
                remainder = remainder - jnp.sum(red_b[level].astype(F32), axis=0)
            back[level] = mm(remainder.astype(BF16), dinv[level], NN)
            src, dst = back.at[level], gath.at[level, g_own]
            for k in range(1, cols):
                send(src, dst, ph_r, me_r, lax.rem(me_c + k, cols))
            keep(src, dst, ph_r)

        arrived(gath.at[level], ph_r)
        if level > 0:
            lo, ph_b = level - 1, phase
            phase += 1
            source = gath[level].reshape(nrhs, bs).astype(BF16)
            products = [mm(source, tiles[lo, slot], NN) for slot in range(slots)]
            for blk in range(rep):
                total = None
                for slot in range(slots):
                    hit = pat[1, lo, slot] // cols == blk
                    term = jnp.where(hit, products[slot], 0.0)
                    total = term if total is None else total + term
                part[levels - 1 + lo, blk] = total.astype(BF16).reshape(groups, gr, bs)
            for k in range(groups):
                for blk in range(rep):
                    g = lax.rem(g_own + k, groups)
                    row = me_c + cols * blk
                    src, dst = part.at[levels - 1 + lo, blk, g], red_b.at[lo, me_r]
                    if k:
                        send(src, dst, ph_b, row, 2 * g + lax.rem(me_c, 2))
                    else:
                        @pl.when(row == me_r)
                        def _(src=src, dst=dst, ph_b=ph_b):
                            keep(src, dst, ph_b)

                        @pl.when(row != me_r)
                        def _(src=src, dst=dst, ph_b=ph_b, row=row):
                            send(src, dst, ph_b, row, me_c)
        out[level] = gath[level]

    phase = 0
    for level in range(1, levels):
        @pl.when(is_owner)
        def _(phase=phase):
            n = rows - 1
            sent(red_b.at[0, pl.ds(0, n)], phase)
            sent(red_f.at[0, pl.ds(0, groups - 1)], phase + 1)

            @pl.when(jnp.logical_not(at_home))
            def _():
                sent(red_b.at[0, 0], phase)

        @pl.when(jnp.logical_not(is_owner))
        def _(phase=phase):
            sent(red_f.at[0, pl.ds(0, groups)], phase + 1)

        phase += 2
    for level in range(levels - 1, -1, -1):
        @pl.when(is_owner)
        def _(phase=phase):
            for k in range(cols - 1):
                sent(gath.at[0, 0], phase)

        phase += 1
        if level > 0:
            sent(red_b.at[0, pl.ds(0, rep * groups - 1)], phase)

            @pl.when(jnp.logical_not(at_home))
            def _(phase=phase):
                sent(red_b.at[0, 0], phase)

            phase += 1


def per_device(rhs, dinv, tiles, pattern):
    levels, _, nrhs, bs = rhs.shape
    rows, cols = lax.axis_size("row"), lax.axis_size("col")
    rep, groups = rows // cols, cols // 2
    gr, slots = nrhs // groups, tiles.shape[2]
    pairs = levels - 1
    phases = 2 * pairs + levels + pairs
    out = pl.pallas_call(
        functools.partial(kernel, (levels, rows, cols, rep, groups, gr, bs)),
        out_shape=jax.ShapeDtypeStruct((levels, groups, gr, bs), F32),
        in_specs=[pl.BlockSpec(memory_space=pltpu.SMEM)] + [pl.BlockSpec(memory_space=pl.ANY)] * 3,
        out_specs=pl.BlockSpec(memory_space=pltpu.VMEM),
        scratch_shapes=[
            pltpu.VMEM((levels, gr, bs), BF16),
            pltpu.VMEM((levels, bs, bs), BF16),
            pltpu.VMEM((pairs, slots, bs, bs), BF16),
            pltpu.SemaphoreType.DMA((3,)),
            pltpu.VMEM((levels, gr, bs), F32),
            pltpu.VMEM((pairs, gr, bs), BF16),
            [pltpu.VMEM((rep, groups, gr, bs), BF16) for _ in range(pairs)],
            pltpu.VMEM((2 * pairs, rep, groups, gr, bs), BF16),
            pltpu.VMEM((pairs, cols, gr, bs), BF16),
            pltpu.VMEM((levels, groups, gr, bs), F32),
            pltpu.VMEM((levels, gr, bs), F32),
            pltpu.VMEM((pairs, rows, gr, bs), BF16),
            pltpu.SemaphoreType.DMA((1,)),
            pltpu.SemaphoreType.DMA((phases,)),
            pltpu.SemaphoreType.DMA((phases,)),
        ],
        compiler_params=pltpu.CompilerParams(
            collective_id=0, has_side_effects=True, vmem_limit_bytes=16 * 2**20
        ),
    )(
        pattern[:, :, 0, :],
        rhs.reshape(levels, groups, gr, bs),
        dinv.reshape(levels, bs, bs),
        tiles.reshape(pairs, slots, bs, bs),
    )
    return out.reshape(levels, 1, nrhs, bs)


def solution(mesh):
    in_specs = (
        P(None, "row", None, None),
        P(None, "row", None, None),
        P(None, "row", "col", None, None),
        P(None, None, "row", "col"),
    )
    return jax.shard_map(
        per_device, mesh=mesh, in_specs=in_specs, out_specs=P(None, "row", None, None), check_vma=False
    )
```

time: 1230 us -> 91.6 us (0.07)
  waiting for transfers between devices: 1190 us -> 0 us
  Pallas kernels: 0 us -> 87.1 us
  between operations: 13.6 us -> 0.01 us
    psum x8 -> x0, waiting for transfers between devices: 1190 us -> none  [the longest x4 591 us: broadcast(): return lax.psum(block, axis)]
    pallas_call x0 -> x1, Pallas kernels: none -> 87.1 us  [per_device(): pl.pallas_call(functools.partial(kernel, (levels, rows, cols, rep, groups...]
  transfers between devices with their start and end apart: 8 -> 0, of which waited for: 8 -> 0; matrix products, arithmetic and copies ran while one was open for 0% -> 0% of each run, Pallas kernels for 0% -> 0%
where the time goes in v1:
time: 91.6 us; the launch traced here: 91.4 us
  Pallas kernels  87.1 us (95%)
  local copies, waits for them, and re-layouts  4.29 us (5%)
    pallas_call x1, Pallas kernels, per_device(): pl.pallas_call(functools.partial(kernel, (levels, rows, cols, rep, groups...  87.1 us
    unnamed x9, local copies, waits for them, and re-layouts  4.29 us

profile of v1, /device:TPU:1, one launch (start us, length us, event | category | flops | bytes accessed | tf_op | source)
XLA Modules:
  0.0 91.4 jit_solution(8175685411778128055)
XLA Ops:
  0.0 0.0 copy-start.3
  0.0 0.7 copy-done.3
  0.7 0.0 copy-start
  0.7 1.0 %copy-done = bf16[2,1,2,256,256]{4,3,2,1,0:T(8,128)(2,1)S(1)} copy-done((bf16[2,1,2,256,256]{4,3,2,1,0:T(8,128)(2,1)S(1)}, bf16[2,1,2,256,256]{4,3,2,1,0:T(8,128)(2,1)}, u32[]{:S(2)}) %copy-start) | copy-done | bytes 524312
  1.7 0.0 copy-start.1
  1.7 1.0 %copy-done.1 = bf16[3,1,256,256]{3,2,1,0:T(8,128)(2,1)S(1)} copy-done((bf16[3,1,256,256]{3,2,1,0:T(8,128)(2,1)S(1)}, bf16[3,1,256,256]{3,2,1,0:T(8,128)(2,1)}, u32[]{:S(2)}) %copy-start.1) | copy-done | bytes 393240
  2.7 0.0 copy-start.2
  2.7 0.9 copy-done.2
  3.6 87.1 %shard_map.46 = f32[3,8,8,256]{3,2,1,0:T(8,128)S(1)} custom-call(s32[2,2,2]{2,1,0:T(2,128)S(1)} %bitcast.11, bf16[3,8,8,256]{3,2,1,0:T(8,128)(2,1)S(1)} %bitcast.10, bf16[3,256,256]{2,1,0:T(8,128)(2,1)S(1)} %bitcast.9, bf16[2,2,256,256]{3,2,1,0:T(8,128)(2,1)S(1)} %bitcast.8), custom_call_target="tpu_custom_call" | custom-call | tf_op jit(solution)/shard_map/pallas_call | solution.py:236
  90.7 0.7 copy.7
Async XLA Ops:
  0.0 0.7 copy-start.3
  0.7 1.0 %copy-start = (bf16[2,1,2,256,256]{4,3,2,1,0:T(8,128)(2,1)S(1)}, bf16[2,1,2,256,256]{4,3,2,1,0:T(8,128)(2,1)}, u32[]{:S(2)}) copy-start(bf16[2,1,2,256,256]{4,3,2,1,0:T(8,128)(2,1)} %param.6) | copy-start | bytes 1572868
  1.7 1.0 %copy-start.1 = (bf16[3,1,256,256]{3,2,1,0:T(8,128)(2,1)S(1)}, bf16[3,1,256,256]{3,2,1,0:T(8,128)(2,1)}, u32[]{:S(2)}) copy-start(bf16[3,1,256,256]{3,2,1,0:T(8,128)(2,1)} %param.5) | copy-start | bytes 1179652
  2.7 0.9 copy-start.2

commit v2 on v1

v2 whole, which is shorter than its diff:
```python
import functools

import jax
import jax.numpy as jnp
from jax import lax
from jax.experimental import pallas as pl
from jax.experimental.pallas import tpu as pltpu
from jax.sharding import PartitionSpec as P

MESH = pl.DeviceIdType.MESH
BF16, F32 = jnp.bfloat16, jnp.float32
NT = (((1,), (1,)), ((), ()))
NN = (((1,), (0,)), ((), ()))


def mm(a, b, dims):
    return lax.dot_general(a, b, dims, preferred_element_type=F32)


def kernel(
    dims,
    pat, rhs_hbm, dinv_hbm, tiles_hbm, out,
    rhs, dinv, tiles, load_sem,
    fwd, own, spread, part, red_f, gath, back, red_b,
    self_sem, send_sem, recv_sem,
):
    levels, rows, cols, rep, groups, gr, bs = dims
    nrhs = groups * gr
    slots = tiles.shape[1]
    me_r, me_c = lax.axis_index("row"), lax.axis_index("col")
    side, g_own = lax.rem(me_r, 2), me_c // 2
    home = lax.rem(me_r, cols)
    blk_own = me_r // cols
    is_owner = lax.rem(me_c, 2) == side
    at_home = home == me_c

    loads = [
        pltpu.make_async_copy(rhs_hbm.at[:, g_own], rhs, load_sem.at[0]),
        pltpu.make_async_copy(dinv_hbm, dinv, load_sem.at[1]),
        pltpu.make_async_copy(tiles_hbm, tiles, load_sem.at[2]),
    ]
    for load in loads:
        load.start()

    barrier = pltpu.get_barrier_semaphore()

    def tell(r, c):
        pl.semaphore_signal(barrier, inc=1, device_id=(r, c), device_id_type=MESH)

    def loop(n, body):
        for k in range(n):
            body(k)

    with jax.named_scope("tell"):
        for blk in range(rep):
            def from_owner(k, blk=blk):
                tell(me_c + cols * blk, 2 * lax.rem(g_own + k, groups) + lax.rem(me_c, 2))

            loop(groups, from_owner)
        loop(groups, lambda k: tell(me_r, 2 * lax.rem(g_own + k, groups) + side))

    with jax.named_scope("meet"):
        @pl.when(is_owner)
        def _():
            loop(cols, lambda k: tell(me_r, lax.rem(me_c + k, cols)))
            loop(rows, lambda k: tell(lax.rem(me_r + k, rows), home))
            pl.semaphore_wait(barrier, rows + cols + groups + rep * groups)

        @pl.when(jnp.logical_not(is_owner))
        def _():
            pl.semaphore_wait(barrier, groups + rep * groups)

    def send(src, dst, phase, r, c):
        pltpu.make_async_remote_copy(
            src_ref=src, dst_ref=dst, send_sem=send_sem.at[phase], recv_sem=recv_sem.at[phase],
            device_id=(r, c), device_id_type=MESH,
        ).start()

    def keep(src, dst, phase):
        pltpu.make_async_copy(src, dst, recv_sem.at[phase]).start()

    def arrived(ref, phase):
        pltpu.make_async_copy(ref, ref, recv_sem.at[phase]).wait()

    def sent(ref, phase):
        pltpu.make_async_copy(ref, ref, send_sem.at[phase]).wait()


    phase = 0
    loads[0].wait()
    loads[1].wait()

    for level in range(levels):
        if level == 0:
            @pl.when(is_owner)
            def _():
                fwd[0] = mm(rhs[0], dinv[0], NT)
        else:
            sp, ph_s, ph_r = level - 1, phase, phase + 1
            phase += 2

            with jax.named_scope("spread"):
                @pl.when(is_owner)
                def _(sp=sp, ph_s=ph_s):
                    own[sp] = fwd[sp].astype(BF16)
                    src, dst = own.at[sp], spread[sp].at[blk_own, g_own]

                    def one(k):
                        send(src, dst, ph_s, lax.rem(me_r + k, rows), home)

                    for k in range(1, rows):
                        one((k + rows // 2 - 1) % (rows - 1) + 1)

                    @pl.when(at_home)
                    def _():
                        keep(src, dst, ph_s)

                    @pl.when(jnp.logical_not(at_home))
                    def _():
                        one(0)

            if level == 1:
                loads[2].wait()
            with jax.named_scope("spread_wait"):
                arrived(spread[sp], ph_s)
            with jax.named_scope("tiles"):
                total = None
                for slot in range(slots):
                    blk = pat[1, sp, slot] // cols
                    source = spread[sp][blk].astype(F32).reshape(nrhs, bs).astype(BF16)
                    product = mm(source, tiles[sp, slot], NT)
                    total = product if total is None else total + product
                part[sp, 0] = total.astype(BF16).reshape(groups, gr, bs)

            def one(k, sp=sp, ph_r=ph_r):
                g = lax.rem(g_own + k, groups)
                send(part.at[sp, 0, g], red_f.at[sp, me_c], ph_r, me_r, 2 * g + side)

            with jax.named_scope("reduce"):
                for k in range(1, groups):
                    one(k)

            @pl.when(jnp.logical_not(is_owner))
            def _(one=one):
                one(0)

            @pl.when(is_owner)
            def _(sp=sp, ph_r=ph_r, level=level):
                keep(part.at[sp, 0, g_own], red_f.at[sp, me_c], ph_r)
                with jax.named_scope("reduce_wait"):
                    arrived(red_f.at[sp], ph_r)
                update = jnp.sum(red_f[sp].astype(F32), axis=0)
                current = rhs[level].astype(F32) - update
                fwd[level] = mm(current.astype(BF16), dinv[level], NT)

    for level in range(levels - 1, -1, -1):
        ph_r = phase
        phase += 1

        @pl.when(is_owner)
        def _(level=level, ph_r=ph_r):
            remainder = fwd[level]
            if level < levels - 1:
                with jax.named_scope("reduce_wait"):
                    arrived(red_b.at[level], ph_r - 1)
                remainder = remainder - jnp.sum(red_b[level].astype(F32), axis=0)
            back[level] = mm(remainder.astype(BF16), dinv[level], NN)
            src, dst = back.at[level], gath.at[level, g_own]
            with jax.named_scope("gather"):
                for k in range(1, cols):
                    send(src, dst, ph_r, me_r, lax.rem(me_c + k, cols))
            keep(src, dst, ph_r)

        with jax.named_scope("gather_wait"):
            arrived(gath.at[level], ph_r)
        if level > 0:
            lo, ph_b = level - 1, phase
            phase += 1
            with jax.named_scope("tiles"):
                source = gath[level].reshape(nrhs, bs).astype(BF16)
                products = [mm(source, tiles[lo, slot], NN) for slot in range(slots)]
                for blk in range(rep):
                    total = None
                    for slot in range(slots):
                        hit = pat[1, lo, slot] // cols == blk
                        term = jnp.where(hit, products[slot], 0.0)
                        total = term if total is None else total + term
                    part[levels - 1 + lo, blk] = total.astype(BF16).reshape(groups, gr, bs)
            with jax.named_scope("reduce"):
                for k in range(groups):
                    for blk in range(rep):
                        g = lax.rem(g_own + k, groups)
                        row = me_c + cols * blk
                        src, dst = part.at[levels - 1 + lo, blk, g], red_b.at[lo, me_r]
                        if k:
                            send(src, dst, ph_b, row, 2 * g + lax.rem(me_c, 2))
                        else:
                            @pl.when(row == me_r)
                            def _(src=src, dst=dst, ph_b=ph_b):
                                keep(src, dst, ph_b)

                            @pl.when(row != me_r)
                            def _(src=src, dst=dst, ph_b=ph_b, row=row):
                                send(src, dst, ph_b, row, me_c)
        out[level] = gath[level]

    with jax.named_scope("drain"):
        phase = 0
        for level in range(1, levels):
            @pl.when(is_owner)
            def _(phase=phase):
                n = rows - 1
                sent(red_b.at[0, pl.ds(0, n)], phase)
                sent(red_f.at[0, pl.ds(0, groups - 1)], phase + 1)

                @pl.when(jnp.logical_not(at_home))
                def _():
                    sent(red_b.at[0, 0], phase)

            @pl.when(jnp.logical_not(is_owner))
            def _(phase=phase):
                sent(red_f.at[0, pl.ds(0, groups)], phase + 1)

            phase += 2
        for level in range(levels - 1, -1, -1):
            @pl.when(is_owner)
            def _(phase=phase):
                for k in range(cols - 1):
                    sent(gath.at[0, 0], phase)

            phase += 1
            if level > 0:
                sent(red_b.at[0, pl.ds(0, rep * groups - 1)], phase)

                @pl.when(jnp.logical_not(at_home))
                def _(phase=phase):
                    sent(red_b.at[0, 0], phase)

                phase += 1


def per_device(rhs, dinv, tiles, pattern):
    levels, _, nrhs, bs = rhs.shape
    rows, cols = lax.axis_size("row"), lax.axis_size("col")
    rep, groups = rows // cols, cols // 2
    gr, slots = nrhs // groups, tiles.shape[2]
    pairs = levels - 1
    phases = 2 * pairs + levels + pairs
    out = pl.pallas_call(
        functools.partial(kernel, (levels, rows, cols, rep, groups, gr, bs)),
        out_shape=jax.ShapeDtypeStruct((levels, groups, gr, bs), F32),
        in_specs=[pl.BlockSpec(memory_space=pltpu.SMEM)] + [pl.BlockSpec(memory_space=pl.ANY)] * 3,
        out_specs=pl.BlockSpec(memory_space=pltpu.VMEM),
        scratch_shapes=[
            pltpu.VMEM((levels, gr, bs), BF16),
            pltpu.VMEM((levels, bs, bs), BF16),
            pltpu.VMEM((pairs, slots, bs, bs), BF16),
            pltpu.SemaphoreType.DMA((3,)),
            pltpu.VMEM((levels, gr, bs), F32),
            pltpu.VMEM((pairs, gr, bs), BF16),
            [pltpu.VMEM((rep, groups, gr, bs), BF16) for _ in range(pairs)],
            pltpu.VMEM((2 * pairs, rep, groups, gr, bs), BF16),
            pltpu.VMEM((pairs, cols, gr, bs), BF16),
            pltpu.VMEM((levels, groups, gr, bs), F32),
            pltpu.VMEM((levels, gr, bs), F32),
            pltpu.VMEM((pairs, rows, gr, bs), BF16),
            pltpu.SemaphoreType.DMA((1,)),
            pltpu.SemaphoreType.DMA((phases,)),
            pltpu.SemaphoreType.DMA((phases,)),
        ],
        compiler_params=pltpu.CompilerParams(
            collective_id=0, has_side_effects=True
        ),
    )(
        pattern[:, :, 0, :],
        rhs.reshape(levels, groups, gr, bs),
        dinv.reshape(levels, bs, bs),
        tiles.reshape(pairs, slots, bs, bs),
    )
    return out.reshape(levels, 1, nrhs, bs)


def solution(mesh):
    in_specs = (
        P(None, "row", None, None),
        P(None, "row", None, None),
        P(None, "row", "col", None, None),
        P(None, None, "row", "col"),
    )
    return jax.shard_map(
        per_device, mesh=mesh, in_specs=in_specs, out_specs=P(None, "row", None, None), check_vma=False
    )
```

time: 91.6 us -> 89.4 us (0.976)
  local copies, waits for them, and re-layouts: 4.29 us -> 1.62 us
    unnamed x9 -> x1, local copies, waits for them, and re-layouts: 4.29 us -> 1.62 us
where the time goes in v2:
time: 89.4 us; the launch traced here: 89.3 us
  Pallas kernels  87.7 us (98%)
  local copies, waits for them, and re-layouts  1.62 us (2%)
    pallas_call x1, Pallas kernels, per_device(): pl.pallas_call(functools.partial(kernel, (levels, rows, cols, rep, groups...  87.7 us

profile of v2, /device:TPU:1, one launch (start us, length us, event | category | flops | bytes accessed | tf_op | source)
XLA Modules:
  0.0 89.3 jit_solution(15078503593482569031)
XLA Ops:
  0.0 87.7 %shard_map.46 = f32[3,8,8,256]{3,2,1,0:T(8,128)} custom-call(s32[2,2,2]{2,1,0:T(2,128)} %bitcast.11, bf16[3,8,8,256]{3,2,1,0:T(8,128)(2,1)} %bitcast.10, bf16[3,256,256]{2,1,0:T(8,128)(2,1)} %bitcast.9, bf16[2,2,256,256]{3,2,1,0:T(8,128)(2,1)} %bitcast.8), custom_call_target="tpu_custom_call" | custom-call | tf_op jit(solution)/shard_map/pallas_call | solution.py:249
  87.7 1.6 %copy.7 = f32[3,1,64,256]{3,2,1,0:T(8,128)} copy(f32[3,1,64,256]{3,2,1,0:T(8,128)} %bitcast.7) | data formatting | bytes 393216

commit v3 on v1

v3 whole, which is shorter than its diff:
```python
import functools

import jax
import jax.numpy as jnp
from jax import lax
from jax.experimental import pallas as pl
from jax.experimental.pallas import tpu as pltpu
from jax.sharding import PartitionSpec as P

MESH = pl.DeviceIdType.MESH
BF16, F32 = jnp.bfloat16, jnp.float32
NT = (((1,), (1,)), ((), ()))
NN = (((1,), (0,)), ((), ()))
NY = 4


def mm(a, b, dims):
    return lax.dot_general(a, b, dims, preferred_element_type=F32)


def ring(k, n):
    return min(k % n, n - k % n)


def add_up(ref, n):
    total = ref[0].astype(F32)
    for k in range(1, n):
        total = total + ref[k].astype(F32)
    return total


def kernel(
    dims,
    pat_hbm, rhs_hbm, dinv_hbm, tiles_hbm, out,
    pat, rhs, dinv, tiles, load_sem,
    fwd, first, own, spread, part, red_f, red_a, part_b, red_b, back, gath, gath_f,
    send_sem, recv_sem,
):
    levels, rows, cols, rep, groups, gr, bs = dims
    nrhs = groups * gr
    slots = tiles.shape[1]
    nx, ny = cols // NY, NY
    me_r, me_c = lax.axis_index("row"), lax.axis_index("col")
    x, y = me_c // ny, lax.rem(me_c, ny)
    home = lax.rem(me_r, cols)
    blk_own = me_r // cols
    at_home = home == me_c
    home_x = home // ny
    is_owner = home_x == x
    barrier = pltpu.get_barrier_semaphore()

    def tell(r, c):
        pl.semaphore_signal(barrier, inc=1, device_id=(r, c), device_id_type=MESH)

    along = sorted(range(rows), key=lambda k: -ring(k // 2, rows // 2))
    plane = sorted(
        ((dx, dy) for dx in range(nx) for dy in range(ny)), key=lambda d: -ring(d[0], nx) - ring(d[1], ny)
    )
    turn = sorted(range(ny), key=lambda k: -ring(k, ny))

    def at_row(k):
        return lax.rem(me_r + k, rows)

    def at_plane(d):
        return lax.rem(x + d[0], nx) * ny + lax.rem(y + d[1], ny)

    for blk in range(rep):
        tell(me_c + cols * blk, me_c)

    loads = [
        pltpu.make_async_copy(rhs_hbm, rhs, load_sem.at[0]),
        pltpu.make_async_copy(dinv_hbm.at[0], dinv.at[0], load_sem.at[1]),
        pltpu.make_async_copy(pat_hbm, pat, load_sem.at[2]),
        pltpu.make_async_copy(tiles_hbm, tiles, load_sem.at[3]),
        pltpu.make_async_copy(dinv_hbm.at[pl.ds(1, levels - 1)], dinv.at[pl.ds(1, levels - 1)], load_sem.at[4]),
    ]
    for load in loads:
        load.start()

    @pl.when(is_owner)
    def _():
        for d in plane:
            tell(me_r, at_plane(d))

    drains = []

    def drain():
        while drains:
            drains.pop(0)()

    def send(src, dst, phase, r, c):
        pltpu.make_async_remote_copy(
            src_ref=src, dst_ref=dst, send_sem=send_sem.at[phase], recv_sem=recv_sem.at[phase],
            device_id=(r, c), device_id_type=MESH,
        ).start()

    def keep(src, dst, phase):
        pltpu.make_async_copy(src, dst, recv_sem.at[phase]).start()

    def arrived(ref, phase):
        pltpu.make_async_copy(ref, ref, recv_sem.at[phase]).wait()

    def sent(units, phase, when=None):
        def wait():
            left = units
            while left:
                n = min(left, rows)
                ref = red_b.at[0, pl.ds(0, n)]
                pltpu.make_async_copy(ref, ref, send_sem.at[phase]).wait()
                left -= n

        if when is None:
            drains.append(wait)
        else:
            drains.append(lambda: pl.when(when)(wait))

    loads[0].wait()
    loads[1].wait()
    phase = 0

    @pl.when(at_home)
    def _():
        first[...] = mm(rhs[0].reshape(nrhs, bs), dinv[0], NT).astype(BF16)
        pl.semaphore_wait(barrier, rows + groups)
        for k in along:
            if k:
                send(first, spread[0].at[blk_own], 0, at_row(k), me_c)
        keep(first, spread[0].at[blk_own], 0)

    @pl.when(jnp.logical_not(at_home))
    def _():
        pl.semaphore_wait(barrier, groups)

    @pl.when(is_owner)
    def _():
        fwd[0] = mm(rhs[0, y], dinv[0], NT)

    loads[2].wait()
    loads[3].wait()
    loads[4].wait()
    sent((rows - 1) * groups, 0, at_home)
    phase = 1

    for level in range(1, levels):
        sp = level - 1
        if level > 1:
            @pl.when(is_owner)
            def _(phase=phase, sp=sp):
                own[sp] = fwd[sp].astype(BF16)
                src, dst = own.at[sp], spread[sp].at[blk_own, y]
                for k in along:
                    if k:
                        send(src, dst, phase, at_row(k), home)

                @pl.when(at_home)
                def _():
                    keep(src, dst, phase)

                @pl.when(jnp.logical_not(at_home))
                def _():
                    send(src, dst, phase, me_r, home)

            drain()
            sent(rows - 1, phase, is_owner)
            sent(1, phase, jnp.logical_and(is_owner, jnp.logical_not(at_home)))
            phase += 1
        arrived(spread[sp], phase - 1)
        total = None
        for slot in range(slots):
            blk = pat[1, sp, slot] // cols
            source = spread[sp][blk].reshape(nrhs, bs)
            product = mm(source, tiles[sp, slot], NT)
            total = product if total is None else total + product
        part[sp] = total.astype(BF16).reshape(groups, gr, bs)
        if level < levels - 1:
            for k in turn:
                g = lax.rem(y + k, groups)
                src, dst = part.at[sp, g], red_f.at[sp, me_c]
                if k:
                    send(src, dst, phase, me_r, home_x * ny + g)
                else:
                    @pl.when(is_owner)
                    def _(src=src, dst=dst, phase=phase):
                        keep(src, dst, phase)

                    @pl.when(jnp.logical_not(is_owner))
                    def _(src=src, dst=dst, phase=phase):
                        send(src, dst, phase, me_r, home_x * ny + y)

            drain()
            sent(groups - 1, phase)
            sent(1, phase, jnp.logical_not(is_owner))

            @pl.when(is_owner)
            def _(sp=sp, level=level, phase=phase):
                arrived(red_f.at[sp], phase)
                current = rhs[level, y].astype(F32) - add_up(red_f.at[sp], cols)
                fwd[level] = mm(current.astype(BF16), dinv[level], NT)

        else:
            for d in plane:
                if d != (0, 0):
                    send(part.at[sp], red_a.at[me_c], phase, me_r, at_plane(d))
            keep(part.at[sp], red_a.at[me_c], phase)
            drain()
            sent((cols - 1) * groups, phase)
            arrived(red_a, phase)
            current = rhs[level].astype(F32) - add_up(red_a, cols)
            remainder = mm(current.astype(BF16).reshape(nrhs, bs), dinv[level], NT)
            solved = mm(remainder.astype(BF16), dinv[level], NN)
            out[level] = solved.reshape(groups, gr, bs)
            source = solved.astype(BF16)
        phase += 1

    for level in range(levels - 2, -1, -1):
        products = [mm(source, tiles[level, slot], NN) for slot in range(slots)]
        for blk in range(rep):
            total = None
            for slot in range(slots):
                hit = pat[1, level, slot] // cols == blk
                term = jnp.where(hit, products[slot], 0.0)
                total = term if total is None else total + term
            part_b[level, blk] = total.astype(BF16).reshape(groups, gr, bs)
        for k in turn:
            for blk in range(rep):
                g, row = lax.rem(y + k, groups), me_c + cols * blk
                src, dst = part_b.at[level, blk, g], red_b.at[level, me_r]
                if k:
                    send(src, dst, phase, row, x * ny + g)
                else:
                    @pl.when(row == me_r)
                    def _(src=src, dst=dst, phase=phase):
                        keep(src, dst, phase)

                    @pl.when(row != me_r)
                    def _(src=src, dst=dst, phase=phase, row=row):
                        send(src, dst, phase, row, me_c)

        drain()
        sent(rep * groups - 1, phase)
        sent(1, phase, jnp.logical_not(at_home))

        @pl.when(is_owner)
        def _(level=level, phase=phase):
            arrived(red_b.at[level], phase)
            remainder = fwd[level] - add_up(red_b.at[level], rows)
            solved = mm(remainder.astype(BF16), dinv[level], NN)
            back[level] = solved
            if level > 0:
                own[levels - 1 + level] = solved.astype(BF16)
                src, dst = own.at[levels - 1 + level], gath.at[level, y]
                for d in plane:
                    if d != (0, 0):
                        send(src, dst, phase + 1, me_r, at_plane(d))
                keep(src, dst, phase + 1)
            src, dst = back.at[level], gath_f.at[level, y]
            for d in plane:
                if d != (0, 0):
                    send(src, dst, phase + 2, me_r, at_plane(d))
            keep(src, dst, phase + 2)

        if level > 0:
            sent(cols - 1, phase + 1, is_owner)
        sent(2 * (cols - 1), phase + 2, is_owner)
        if level > 0:
            arrived(gath.at[level], phase + 1)
            source = gath[level].reshape(nrhs, bs)
        phase += 3

    drain()
    for level in range(levels - 2, -1, -1):
        arrived(gath_f.at[level], phase - 3 * level - 1)
        out[level] = gath_f[level]


def per_device(rhs, dinv, tiles, pattern):
    levels, _, nrhs, bs = rhs.shape
    rows, cols = lax.axis_size("row"), lax.axis_size("col")
    rep, groups = rows // cols, NY
    gr, slots = nrhs // groups, tiles.shape[2]
    pairs = levels - 1
    phases = 2 * pairs + 3 * pairs
    out = pl.pallas_call(
        functools.partial(kernel, (levels, rows, cols, rep, groups, gr, bs)),
        out_shape=jax.ShapeDtypeStruct((levels, groups, gr, bs), F32),
        in_specs=[pl.BlockSpec(memory_space=pl.ANY)] * 4,
        out_specs=pl.BlockSpec(memory_space=pltpu.VMEM),
        scratch_shapes=[
            pltpu.SMEM((2, pairs, slots), jnp.int32),
            pltpu.VMEM((levels, groups, gr, bs), BF16),
            pltpu.VMEM((levels, bs, bs), BF16),
            pltpu.VMEM((pairs, slots, bs, bs), BF16),
            pltpu.SemaphoreType.DMA((5,)),
            pltpu.VMEM((pairs, gr, bs), F32),
            pltpu.VMEM((nrhs, bs), BF16),
            pltpu.VMEM((2 * pairs, gr, bs), BF16),
            [pltpu.VMEM((rep, nrhs, bs), BF16)]
            + [pltpu.VMEM((rep, groups, gr, bs), BF16) for _ in range(pairs - 1)],
            pltpu.VMEM((pairs, groups, gr, bs), BF16),
            pltpu.VMEM((pairs, cols, gr, bs), BF16),
            pltpu.VMEM((cols, groups, gr, bs), BF16),
            pltpu.VMEM((pairs, rep, groups, gr, bs), BF16),
            pltpu.VMEM((pairs, rows, gr, bs), BF16),
            pltpu.VMEM((pairs, gr, bs), F32),
            pltpu.VMEM((pairs, groups, gr, bs), BF16),
            pltpu.VMEM((pairs, groups, gr, bs), F32),
            pltpu.SemaphoreType.DMA((phases,)),
            pltpu.SemaphoreType.DMA((phases,)),
        ],
        compiler_params=pltpu.CompilerParams(
            collective_id=0, has_side_effects=True
        ),
    )(
        pattern[:, :, 0, :],
        rhs.reshape(levels, groups, gr, bs),
        dinv.reshape(levels, bs, bs),
        tiles.reshape(pairs, slots, bs, bs),
    )
    return out.reshape(levels, 1, nrhs, bs)


def solution(mesh):
    in_specs = (
        P(None, "row", None, None),
        P(None, "row", None, None),
        P(None, "row", "col", None, None),
        P(None, None, "row", "col"),
    )
    return jax.shard_map(
        per_device, mesh=mesh, in_specs=in_specs, out_specs=P(None, "row", None, None), check_vma=False
    )
```

time: 91.6 us -> 75.1 us (0.82)
  Pallas kernels: 87.1 us -> 72.4 us
  local copies, waits for them, and re-layouts: 4.29 us -> 1.62 us
    pallas_call x1, Pallas kernels: 87.1 us -> 72.4 us  [per_device(): pl.pallas_call(functools.partial(kernel, (levels, rows, cols, rep, groups...]
    unnamed x9 -> x1, local copies, waits for them, and re-layouts: 4.29 us -> 1.62 us
where the time goes in v3:
time: 75.1 us; the launch traced here: 74 us
  Pallas kernels  72.4 us (96%)
  local copies, waits for them, and re-layouts  1.62 us (2%)
    pallas_call x1, Pallas kernels, per_device(): pl.pallas_call(functools.partial(kernel, (levels, rows, cols, rep, groups...  72.4 us
    unnamed x1, local copies, waits for them, and re-layouts  1.62 us

profile of v3, /device:TPU:1, one launch (start us, length us, event | category | flops | bytes accessed | tf_op | source)
XLA Modules:
  0.0 74.0 jit_solution(12448080679790721547)
XLA Ops:
  0.0 72.4 %shard_map.46 = f32[3,4,16,256]{3,2,1,0:T(8,128)} custom-call(s32[2,2,2]{2,1,0:T(2,128)} %bitcast.11, bf16[3,4,16,256]{3,2,1,0:T(8,128)(2,1)} %bitcast.10, bf16[3,256,256]{2,1,0:T(8,128)(2,1)} %bitcast.9, bf16[2,2,256,256]{3,2,1,0:T(8,128)(2,1)} %bitcast.8), custom_call_target="tpu_custom_call" | custom-call | tf_op jit(solution)/shard_map/pallas_call | solution.py:283
  72.4 1.6 %copy.7 = f32[3,1,64,256]{3,2,1,0:T(8,128)} copy(f32[3,1,64,256]{3,2,1,0:T(8,128)} %bitcast.7) | data formatting | bytes 393216

commit v4 on v3

--- a/solution.py
+++ b/solution.py
@@ -45,8 +45,8 @@
     home = lax.rem(me_r, cols)
     blk_own = me_r // cols
     at_home = home == me_c
-    home_x = home // ny
-    is_owner = home_x == x
+    home_y = lax.rem(home, ny)
+    is_owner = home_y == y
     barrier = pltpu.get_barrier_semaphore()
 
     def tell(r, c):
@@ -56,7 +56,7 @@
     plane = sorted(
         ((dx, dy) for dx in range(nx) for dy in range(ny)), key=lambda d: -ring(d[0], nx) - ring(d[1], ny)
     )
-    turn = sorted(range(ny), key=lambda k: -ring(k, ny))
+    turn = sorted(range(nx), key=lambda k: -ring(k, nx))
 
     def at_row(k):
         return lax.rem(me_r + k, rows)
@@ -133,7 +133,7 @@
 
     @pl.when(is_owner)
     def _():
-        fwd[0] = mm(rhs[0, y], dinv[0], NT)
+        fwd[0] = mm(rhs[0, x], dinv[0], NT)
 
     loads[2].wait()
     loads[3].wait()
@@ -147,7 +147,7 @@
             @pl.when(is_owner)
             def _(phase=phase, sp=sp):
                 own[sp] = fwd[sp].astype(BF16)
-                src, dst = own.at[sp], spread[sp].at[blk_own, y]
+                src, dst = own.at[sp], spread[sp].at[blk_own, x]
                 for k in along:
                     if k:
                         send(src, dst, phase, at_row(k), home)
@@ -174,10 +174,10 @@
         part[sp] = total.astype(BF16).reshape(groups, gr, bs)
         if level < levels - 1:
             for k in turn:
-                g = lax.rem(y + k, groups)
+                g = lax.rem(x + k, groups)
                 src, dst = part.at[sp, g], red_f.at[sp, me_c]
                 if k:
-                    send(src, dst, phase, me_r, home_x * ny + g)
+                    send(src, dst, phase, me_r, g * ny + home_y)
                 else:
                     @pl.when(is_owner)
                     def _(src=src, dst=dst, phase=phase):
@@ -185,7 +185,7 @@
 
                     @pl.when(jnp.logical_not(is_owner))
                     def _(src=src, dst=dst, phase=phase):
-                        send(src, dst, phase, me_r, home_x * ny + y)
+                        send(src, dst, phase, me_r, x * ny + home_y)
 
             drain()
             sent(groups - 1, phase)
@@ -194,7 +194,7 @@
             @pl.when(is_owner)
             def _(sp=sp, level=level, phase=phase):
                 arrived(red_f.at[sp], phase)
-                current = rhs[level, y].astype(F32) - add_up(red_f.at[sp], cols)
+                current = rhs[level, x].astype(F32) - add_up(red_f.at[sp], cols)
                 fwd[level] = mm(current.astype(BF16), dinv[level], NT)
 
         else:
@@ -212,6 +212,13 @@
             source = solved.astype(BF16)
         phase += 1
 
+    def gather_f(level, phase):
+        src, dst = back.at[level], gath_f.at[level, x]
+        for d in plane:
+            if d != (0, 0):
+                send(src, dst, phase, me_r, at_plane(d))
+        keep(src, dst, phase)
+
     for level in range(levels - 2, -1, -1):
         products = [mm(source, tiles[level, slot], NN) for slot in range(slots)]
         for blk in range(rep):
@@ -223,10 +230,10 @@
             part_b[level, blk] = total.astype(BF16).reshape(groups, gr, bs)
         for k in turn:
             for blk in range(rep):
-                g, row = lax.rem(y + k, groups), me_c + cols * blk
+                g, row = lax.rem(x + k, groups), me_c + cols * blk
                 src, dst = part_b.at[level, blk, g], red_b.at[level, me_r]
                 if k:
-                    send(src, dst, phase, row, x * ny + g)
+                    send(src, dst, phase, row, g * ny + y)
                 else:
                     @pl.when(row == me_r)
                     def _(src=src, dst=dst, phase=phase):
@@ -236,7 +243,14 @@
                     def _(src=src, dst=dst, phase=phase, row=row):
                         send(src, dst, phase, row, me_c)
 
+        if level < levels - 2:
+            @pl.when(is_owner)
+            def _(level=level, phase=phase):
+                gather_f(level + 1, phase - 1)
+
         drain()
+        if level < levels - 2:
+            sent(2 * (cols - 1), phase - 1, is_owner)
         sent(rep * groups - 1, phase)
         sent(1, phase, jnp.logical_not(at_home))
 
@@ -248,20 +262,18 @@
             back[level] = solved
             if level > 0:
                 own[levels - 1 + level] = solved.astype(BF16)
-                src, dst = own.at[levels - 1 + level], gath.at[level, y]
+                src, dst = own.at[levels - 1 + level], gath.at[level, x]
                 for d in plane:
                     if d != (0, 0):
                         send(src, dst, phase + 1, me_r, at_plane(d))
                 keep(src, dst, phase + 1)
-            src, dst = back.at[level], gath_f.at[level, y]
-            for d in plane:
-                if d != (0, 0):
-                    send(src, dst, phase + 2, me_r, at_plane(d))
-            keep(src, dst, phase + 2)
+            if level == 0:
+                gather_f(0, phase + 2)
 
         if level > 0:
             sent(cols - 1, phase + 1, is_owner)
-        sent(2 * (cols - 1), phase + 2, is_owner)
+        if level == 0:
+            sent(2 * (cols - 1), phase + 2, is_owner)
         if level > 0:
             arrived(gath.at[level], phase + 1)
             source = gath[level].reshape(nrhs, bs)
@@ -276,7 +288,7 @@
 def per_device(rhs, dinv, tiles, pattern):
     levels, _, nrhs, bs = rhs.shape
     rows, cols = lax.axis_size("row"), lax.axis_size("col")
-    rep, groups = rows // cols, NY
+    rep, groups = rows // cols, cols // NY
     gr, slots = nrhs // groups, tiles.shape[2]
     pairs = levels - 1
     phases = 2 * pairs + 3 * pairs
@@ -308,13 +320,18 @@
             pltpu.SemaphoreType.DMA((phases,)),
         ],
         compiler_params=pltpu.CompilerParams(
-            collective_id=0, has_side_effects=True
+            collective_id=0, has_side_effects=True, vmem_limit_bytes=16 * 2**20
         ),
     )(
-        pattern[:, :, 0, :],
-        rhs.reshape(levels, groups, gr, bs),
-        dinv.reshape(levels, bs, bs),
-        tiles.reshape(pairs, slots, bs, bs),
+        *[
+            pltpu.with_memory_space_constraint(a, pltpu.HBM)
+            for a in (
+                pattern[:, :, 0, :],
+                rhs.reshape(levels, groups, gr, bs),
+                dinv.reshape(levels, bs, bs),
+                tiles.reshape(pairs, slots, bs, bs),
+            )
+        ]
     )
     return out.reshape(levels, 1, nrhs, bs)
 

time: 75.1 us -> 72.9 us (0.971); the launches traced: 74 us -> 72.8 us
  local copies, waits for them, and re-layouts: 1.62 us -> 0.68 us
    unnamed x1, local copies, waits for them, and re-layouts: 1.62 us -> 0.68 us
where the time goes in v4:
time: 72.9 us; the launch traced here: 72.8 us
  Pallas kernels  72.1 us (99%)
    pallas_call x1, Pallas kernels, per_device(): pl.pallas_call(functools.partial(kernel, (levels, rows, cols, rep, groups...  72.1 us

profile of v4, /device:TPU:1, one launch (start us, length us, event | category | flops | bytes accessed | tf_op | source)
XLA Modules:
  0.0 72.8 jit_solution(11235810907447802444)
XLA Ops:
  0.0 72.1 %shard_map.46 = f32[3,4,16,256]{3,2,1,0:T(8,128)S(1)} custom-call(s32[2,2,2]{2,1,0:T(2,128)} %bitcast.11, bf16[3,4,16,256]{3,2,1,0:T(8,128)(2,1)} %bitcast.10, bf16[3,256,256]{2,1,0:T(8,128)(2,1)} %bitcast.9, bf16[2,2,256,256]{3,2,1,0:T(8,128)(2,1)} %bitcast.8), custom_call_target="tpu_custom_call" | custom-call | tf_op jit(solution)/shard_map/pallas_call | solution.py:295
  72.1 0.7 copy.7

commit v5 on v3

v5 whole, which is shorter than its diff:
```python
import functools

import jax
import jax.numpy as jnp
from jax import lax
from jax.experimental import pallas as pl
from jax.experimental.pallas import tpu as pltpu
from jax.sharding import PartitionSpec as P

MESH = pl.DeviceIdType.MESH
BF16, F32 = jnp.bfloat16, jnp.float32
NT = (((1,), (1,)), ((), ()))
NN = (((1,), (0,)), ((), ()))
NY = 4
GROUPS = 1
PARTS = 2


def mm(a, b, dims):
    return lax.dot_general(a, b, dims, preferred_element_type=F32)


def ring(k, n):
    return min(k % n, n - k % n)


def add_up(ref, n):
    total = ref[0].astype(F32)
    for k in range(1, n):
        total = total + ref[k].astype(F32)
    return total


def kernel(
    dims,
    pat_hbm, rhs_hbm, dinv_hbm, tiles_hbm, out,
    pat, rhs, dinv, tiles, load_sem,
    fwd, first, own, spread, part, red_f, red_a, part_b, red_b, gath,
    send_sem, recv_sem,
):
    levels, rows, cols, rep, parts, groups, gr, bs = dims
    nrhs = groups * gr
    slots = tiles.shape[1]
    nx, ny = cols // NY, NY
    me_r, me_c = lax.axis_index("row"), lax.axis_index("col")
    x, y = me_c // ny, lax.rem(me_c, ny)
    home = lax.rem(me_r, cols)
    blk_own = me_r // cols
    at_home = home == me_c
    home_x, home_y = home // ny, lax.rem(home, ny)
    g_own = lax.rem(x + nx - home_x, nx)
    is_owner = jnp.logical_and(home_y == y, g_own < groups)
    g_own = jnp.minimum(g_own, groups - 1)
    barrier = pltpu.get_barrier_semaphore()

    def tell(r, c):
        pl.semaphore_signal(barrier, inc=1, device_id=(r, c), device_id_type=MESH)

    along = sorted(range(rows), key=lambda k: -ring(k // 2, rows // 2))
    plane = sorted(
        ((dx, dy) for dx in range(nx) for dy in range(ny)), key=lambda d: -ring(d[0], nx) - ring(d[1], ny)
    )

    def at_row(k):
        return lax.rem(me_r + k, rows)

    def at_plane(d):
        return lax.rem(x + d[0], nx) * ny + lax.rem(y + d[1], ny)

    for blk in range(rep):
        tell(me_c + cols * blk, me_c)

    loads = [
        pltpu.make_async_copy(rhs_hbm, rhs, load_sem.at[0]),
        pltpu.make_async_copy(dinv_hbm.at[0], dinv.at[0], load_sem.at[1]),
        pltpu.make_async_copy(pat_hbm, pat, load_sem.at[2]),
        pltpu.make_async_copy(tiles_hbm, tiles, load_sem.at[3]),
        pltpu.make_async_copy(dinv_hbm.at[pl.ds(1, levels - 1)], dinv.at[pl.ds(1, levels - 1)], load_sem.at[4]),
    ]
    for load in loads:
        load.start()

    @pl.when(is_owner)
    def _():
        for d in plane:
            tell(me_r, at_plane(d))

    waits = []

    def drain(lag):
        while len(waits) > lag:
            for wait in waits.pop(0):
                wait()

    def send(src, dst, h, phase, r, c):
        pltpu.make_async_remote_copy(
            src_ref=src, dst_ref=dst, send_sem=send_sem.at[h, phase], recv_sem=recv_sem.at[h, phase],
            device_id=(r, c), device_id_type=MESH,
        ).start()

    def keep(src, dst, h, phase):
        pltpu.make_async_copy(src, dst, recv_sem.at[h, phase]).start()

    def arrived(ref, h, phase):
        pltpu.make_async_copy(ref, ref, recv_sem.at[h, phase]).wait()

    def sent(phase, *pieces):
        def wait(h, units, when):
            def act():
                left = units
                while left:
                    n = min(left, rows)
                    ref = red_b.at[0, 0, pl.ds(0, n)]
                    pltpu.make_async_copy(ref, ref, send_sem.at[h, phase]).wait()
                    left -= n

            return act if when is None else lambda: pl.when(when)(act)

        waits.append([wait(h, *piece) for h in range(parts) for piece in pieces])

    loads[0].wait()
    loads[1].wait()
    phase = 0

    @pl.when(at_home)
    def _():
        solved = mm(rhs[0].reshape(parts * nrhs, bs), dinv[0], NT)
        first[...] = solved.astype(BF16).reshape(parts, nrhs, bs)
        pl.semaphore_wait(barrier, rows + groups)
        for h in range(parts):
            src, dst = first.at[h], spread[0][h].at[blk_own]
            for k in along:
                if k:
                    send(src, dst, h, 0, at_row(k), me_c)
            keep(src, dst, h, 0)

    @pl.when(jnp.logical_not(at_home))
    def _():
        pl.semaphore_wait(barrier, groups)

    @pl.when(is_owner)
    def _():
        for h in range(parts):
            fwd[h, 0] = mm(rhs[0, h, g_own], dinv[0], NT)

    loads[2].wait()
    loads[3].wait()
    loads[4].wait()
    sent(0, ((rows - 1) * groups, at_home))
    phase = 1

    for level in range(1, levels):
        sp = level - 1
        if level > 1:
            @pl.when(is_owner)
            def _(phase=phase, sp=sp):
                for h in range(parts):
                    arrived(red_f.at[h, sp - 1], h, phase - 1)
                    current = rhs[sp, h, g_own].astype(F32) - add_up(red_f.at[h, sp - 1], cols)
                    solved = mm(current.astype(BF16), dinv[sp], NT)
                    fwd[h, sp] = solved
                    own[h, sp] = solved.astype(BF16)
                    src, dst = own.at[h, sp], spread[sp][h].at[blk_own, g_own]
                    for k in along:
                        if k:
                            send(src, dst, h, phase, at_row(k), home)

                    @pl.when(at_home)
                    def _(src=src, dst=dst, h=h):
                        keep(src, dst, h, phase)

                    @pl.when(jnp.logical_not(at_home))
                    def _(src=src, dst=dst, h=h):
                        send(src, dst, h, phase, me_r, home)

            sent(phase, (rows - 1, is_owner), (1, jnp.logical_and(is_owner, jnp.logical_not(at_home))))
            drain(2)
            phase += 1
        for h in range(parts):
            arrived(spread[sp][h], h, phase - 1)
            total = None
            for slot in range(slots):
                blk = pat[1, sp, slot] // cols
                source = spread[sp][h][blk].reshape(nrhs, bs)
                product = mm(source, tiles[sp, slot], NT)
                total = product if total is None else total + product
            part[h, sp] = total.astype(BF16).reshape(groups, gr, bs)
            if level < levels - 1:
                for g in range(groups):
                    src, dst = part.at[h, sp, g], red_f.at[h, sp, me_c]
                    col = lax.rem(home_x + g, nx) * ny + home_y

                    @pl.when(col == me_c)
                    def _(src=src, dst=dst, phase=phase, h=h):
                        keep(src, dst, h, phase)

                    @pl.when(col != me_c)
                    def _(src=src, dst=dst, phase=phase, h=h, col=col):
                        send(src, dst, h, phase, me_r, col)

            else:
                for d in plane:
                    if d != (0, 0):
                        send(part.at[h, sp], red_a.at[h, me_c], h, phase, me_r, at_plane(d))
                keep(part.at[h, sp], red_a.at[h, me_c], h, phase)

        if level < levels - 1:
            sent(phase, (groups - 1, None), (1, jnp.logical_not(is_owner)))
        else:
            sent(phase, ((cols - 1) * groups, None))
        drain(2)
        phase += 1

    for level in range(levels - 2, -1, -1):
        for h in range(parts):
            if level == levels - 2:
                arrived(red_a.at[h], h, phase - 1)
                current = rhs[level + 1, h].astype(F32) - add_up(red_a.at[h], cols)
                remainder = mm(current.astype(BF16).reshape(nrhs, bs), dinv[level + 1], NT)
                solved = mm(remainder.astype(BF16), dinv[level + 1], NN)
                out[level + 1, h] = solved.reshape(groups, gr, bs)
                source = solved.astype(BF16)
            else:
                arrived(gath.at[h, level + 1], h, phase - 1)
                source = gath[h, level + 1].reshape(nrhs, bs)
            products = [mm(source, tiles[level, slot], NN) for slot in range(slots)]
            for blk in range(rep):
                total = None
                for slot in range(slots):
                    hit = pat[1, level, slot] // cols == blk
                    term = jnp.where(hit, products[slot], 0.0)
                    total = term if total is None else total + term
                part_b[h, level, blk] = total.astype(BF16).reshape(groups, gr, bs)
            for g in range(groups - 1, -1, -1):
                for blk in range(rep):
                    row = me_c + cols * blk
                    src, dst = part_b.at[h, level, blk, g], red_b.at[h, level, me_r]
                    if g:
                        send(src, dst, h, phase, row, lax.rem(x + g, nx) * ny + y)
                    else:
                        @pl.when(row == me_r)
                        def _(src=src, dst=dst, phase=phase, h=h):
                            keep(src, dst, h, phase)

                        @pl.when(row != me_r)
                        def _(src=src, dst=dst, phase=phase, row=row, h=h):
                            send(src, dst, h, phase, row, me_c)

            if level < levels - 2:
                out[level + 1, h] = gath[h, level + 1].astype(F32)

        sent(phase, (rep * groups - 1, None), (1, jnp.logical_not(at_home)))
        drain(2)

        @pl.when(is_owner)
        def _(level=level, phase=phase):
            for h in range(parts):
                arrived(red_b.at[h, level], h, phase)
                remainder = fwd[h, level] - add_up(red_b.at[h, level], rows)
                solved = mm(remainder.astype(BF16), dinv[level], NN)
                own[h, levels - 1 + level] = solved.astype(BF16)
                src, dst = own.at[h, levels - 1 + level], gath.at[h, level, g_own]
                for d in plane:
                    if d != (0, 0):
                        send(src, dst, h, phase + 1, me_r, at_plane(d))
                keep(src, dst, h, phase + 1)

        sent(phase + 1, (cols - 1, is_owner))
        drain(1 if level == 0 else 2)
        phase += 2

    for h in range(parts):
        arrived(gath.at[h, 0], h, phase - 1)
        out[0, h] = gath[h, 0].astype(F32)
    drain(0)


def per_device(rhs, dinv, tiles, pattern):
    levels, _, nrhs, bs = rhs.shape
    rows, cols = lax.axis_size("row"), lax.axis_size("col")
    rep, parts, groups = rows // cols, PARTS, GROUPS
    gr, slots = nrhs // (parts * groups), tiles.shape[2]
    pairs = levels - 1
    phases = 2 * pairs + 2 * pairs
    out = pl.pallas_call(
        functools.partial(kernel, (levels, rows, cols, rep, parts, groups, gr, bs)),
        out_shape=jax.ShapeDtypeStruct((levels, parts, groups, gr, bs), F32),
        in_specs=[pl.BlockSpec(memory_space=pl.ANY)] * 4,
        out_specs=pl.BlockSpec(memory_space=pltpu.VMEM),
        scratch_shapes=[
            pltpu.SMEM((2, pairs, slots), jnp.int32),
            pltpu.VMEM((levels, parts, groups, gr, bs), BF16),
            pltpu.VMEM((levels, bs, bs), BF16),
            pltpu.VMEM((pairs, slots, bs, bs), BF16),
            pltpu.SemaphoreType.DMA((5,)),
            pltpu.VMEM((parts, pairs, gr, bs), F32),
            pltpu.VMEM((parts, groups * gr, bs), BF16),
            pltpu.VMEM((parts, 2 * pairs, gr, bs), BF16),
            [[pltpu.VMEM((rep, groups * gr, bs), BF16) for _ in range(parts)]]
            + [[pltpu.VMEM((rep, groups, gr, bs), BF16) for _ in range(parts)] for _ in range(pairs - 1)],
            pltpu.VMEM((parts, pairs, groups, gr, bs), BF16),
            pltpu.VMEM((parts, pairs, cols, gr, bs), BF16),
            pltpu.VMEM((parts, cols, groups, gr, bs), BF16),
            pltpu.VMEM((parts, pairs, rep, groups, gr, bs), BF16),
            pltpu.VMEM((parts, pairs, rows, gr, bs), BF16),
            pltpu.VMEM((parts, pairs, groups, gr, bs), BF16),
            pltpu.SemaphoreType.DMA((parts, phases)),
            pltpu.SemaphoreType.DMA((parts, phases)),
        ],
        compiler_params=pltpu.CompilerParams(
            collective_id=0, has_side_effects=True, vmem_limit_bytes=16 * 2**20
        ),
    )(
        *[
            pltpu.with_memory_space_constraint(a, pltpu.HBM)
            for a in (
                pattern[:, :, 0, :],
                rhs.reshape(levels, parts, groups, gr, bs),
                dinv.reshape(levels, bs, bs),
                tiles.reshape(pairs, slots, bs, bs),
            )
        ]
    )
    return out.reshape(levels, 1, nrhs, bs)


def solution(mesh):
    in_specs = (
        P(None, "row", None, None),
        P(None, "row", None, None),
        P(None, "row", "col", None, None),
        P(None, None, "row", "col"),
    )
    return jax.shard_map(
        per_device, mesh=mesh, in_specs=in_specs, out_specs=P(None, "row", None, None), check_vma=False
    )
```

time: 75.1 us -> 65.9 us (0.88)
  Pallas kernels: 72.4 us -> 64.1 us
  local copies, waits for them, and re-layouts: 1.62 us -> 0.68 us
    pallas_call x1, Pallas kernels: 72.4 us -> 64.1 us  [per_device(): pl.pallas_call(functools.partial(kernel, (levels, rows, cols, rep, parts,...]
    unnamed x1, local copies, waits for them, and re-layouts: 1.62 us -> 0.68 us
where the time goes in v5:
time: 65.9 us; the launch traced here: 64.8 us
  Pallas kernels  64.1 us (97%)
  local copies, waits for them, and re-layouts  0.68 us (1%)
    pallas_call x1, Pallas kernels, per_device(): pl.pallas_call(functools.partial(kernel, (levels, rows, cols, rep, parts,...  64.1 us

profile of v5, /device:TPU:1, one launch (start us, length us, event | category | flops | bytes accessed | tf_op | source)
XLA Modules:
  0.0 64.8 jit_solution(7134963721932272354)
XLA Ops:
  0.0 64.1 %shard_map.46 = f32[3,2,1,32,256]{4,3,2,1,0:T(8,128)S(1)} custom-call(s32[2,2,2]{2,1,0:T(2,128)} %bitcast.11, bf16[3,2,1,32,256]{4,3,2,1,0:T(8,128)(2,1)} %bitcast.10, bf16[3,256,256]{2,1,0:T(8,128)(2,1)} %bitcast.9, bf16[2,2,256,256]{3,2,1,0:T(8,128)(2,1)} %bitcast.8), custom_call_target="tpu_custom_call" | custom-call | tf_op jit(solution)/shard_map/pallas_call | solution.py:285
  64.1 0.7 %copy.7 = f32[3,1,64,256]{3,2,1,0:T(8,128)} copy(f32[3,1,64,256]{3,2,1,0:T(8,128)S(1)} %bitcast.7) | data formatting | bytes 393216

commit v6 on v5

--- a/solution.py
+++ b/solution.py
@@ -13,7 +13,7 @@
 NN = (((1,), (0,)), ((), ()))
 NY = 4
 GROUPS = 1
-PARTS = 2
+PARTS = 4
 
 
 def mm(a, b, dims):

time: 65.9 us -> 65.4 us (level)
  no operation moved by 1% of the time
where the time goes in v6:
time: 65.4 us; the launch traced here: 64.4 us
  Pallas kernels  63.8 us (98%)
  local copies, waits for them, and re-layouts  0.68 us (1%)
    pallas_call x1, Pallas kernels, per_device(): pl.pallas_call(functools.partial(kernel, (levels, rows, cols, rep, parts,...  63.8 us

profile of v6, /device:TPU:1, one launch (start us, length us, event | category | flops | bytes accessed | tf_op | source)
XLA Modules:
  0.0 64.4 jit_solution(10244916373157469708)
XLA Ops:
  0.0 63.8 %shard_map.46 = f32[3,4,1,16,256]{4,3,2,1,0:T(8,128)S(1)} custom-call(s32[2,2,2]{2,1,0:T(2,128)} %bitcast.11, bf16[3,4,1,16,256]{4,3,2,1,0:T(8,128)(2,1)} %bitcast.10, bf16[3,256,256]{2,1,0:T(8,128)(2,1)} %bitcast.9, bf16[2,2,256,256]{3,2,1,0:T(8,128)(2,1)} %bitcast.8), custom_call_target="tpu_custom_call" | custom-call | tf_op jit(solution)/shard_map/pallas_call | solution.py:285
  63.8 0.7 %copy.7 = f32[3,1,64,256]{3,2,1,0:T(8,128)} copy(f32[3,1,64,256]{3,2,1,0:T(8,128)S(1)} %bitcast.7) | data formatting | bytes 393216

commit v7 on v6

--- a/solution.py
+++ b/solution.py
@@ -53,12 +53,20 @@
     g_own = jnp.minimum(g_own, groups - 1)
     barrier = pltpu.get_barrier_semaphore()
 
+    def each(body):
+        def step(h, carry):
+            body(h)
+            return carry
+
+        lax.fori_loop(0, parts, step, 0)
+
+
     def tell(r, c):
         pl.semaphore_signal(barrier, inc=1, device_id=(r, c), device_id_type=MESH)
 
     along = sorted(range(rows), key=lambda k: -ring(k // 2, rows // 2))
     plane = sorted(
-        ((dx, dy) for dx in range(nx) for dy in range(ny)), key=lambda d: -ring(d[0], nx) - ring(d[1], ny)
+        ((dx, dy) for dx in range(nx) for dy in range(ny)), key=lambda d: -2 * ring(d[1], ny) - ring(d[0], nx)
     )
 
     def at_row(k):
@@ -127,8 +135,9 @@
         solved = mm(rhs[0].reshape(parts * nrhs, bs), dinv[0], NT)
         first[...] = solved.astype(BF16).reshape(parts, nrhs, bs)
         pl.semaphore_wait(barrier, rows + groups)
-        for h in range(parts):
-            src, dst = first.at[h], spread[0][h].at[blk_own]
+        @each
+        def _(h, phase=phase):
+            src, dst = first.at[h], spread[0].at[h, blk_own]
             for k in along:
                 if k:
                     send(src, dst, h, 0, at_row(k), me_c)
@@ -140,7 +149,8 @@
 
     @pl.when(is_owner)
     def _():
-        for h in range(parts):
+        @each
+        def _(h, phase=phase):
             fwd[h, 0] = mm(rhs[0, h, g_own], dinv[0], NT)
 
     loads[2].wait()
@@ -154,13 +164,14 @@
         if level > 1:
             @pl.when(is_owner)
             def _(phase=phase, sp=sp):
-                for h in range(parts):
+                @each
+                def _(h, phase=phase):
                     arrived(red_f.at[h, sp - 1], h, phase - 1)
                     current = rhs[sp, h, g_own].astype(F32) - add_up(red_f.at[h, sp - 1], cols)
                     solved = mm(current.astype(BF16), dinv[sp], NT)
                     fwd[h, sp] = solved
                     own[h, sp] = solved.astype(BF16)
-                    src, dst = own.at[h, sp], spread[sp][h].at[blk_own, g_own]
+                    src, dst = own.at[h, sp], spread[sp].at[h, blk_own, g_own]
                     for k in along:
                         if k:
                             send(src, dst, h, phase, at_row(k), home)
@@ -176,12 +187,16 @@
             sent(phase, (rows - 1, is_owner), (1, jnp.logical_and(is_owner, jnp.logical_not(at_home))))
             drain(2)
             phase += 1
-        for h in range(parts):
-            arrived(spread[sp][h], h, phase - 1)
+        @each
+        def _(h, phase=phase):
+            arrived(spread[sp].at[h], h, phase - 1)
             total = None
             for slot in range(slots):
                 blk = pat[1, sp, slot] // cols
-                source = spread[sp][h][blk].reshape(nrhs, bs)
+                source = spread[sp][h, 0]
+                for other in range(1, rep):
+                    source = jnp.where(blk == other, spread[sp][h, other], source)
+                source = source.reshape(nrhs, bs)
                 product = mm(source, tiles[sp, slot], NT)
                 total = product if total is None else total + product
             part[h, sp] = total.astype(BF16).reshape(groups, gr, bs)
@@ -212,7 +227,8 @@
         phase += 1
 
     for level in range(levels - 2, -1, -1):
-        for h in range(parts):
+        @each
+        def _(h, phase=phase):
             if level == levels - 2:
                 arrived(red_a.at[h], h, phase - 1)
                 current = rhs[level + 1, h].astype(F32) - add_up(red_a.at[h], cols)
@@ -254,7 +270,8 @@
 
         @pl.when(is_owner)
         def _(level=level, phase=phase):
-            for h in range(parts):
+            @each
+            def _(h, phase=phase):
                 arrived(red_b.at[h, level], h, phase)
                 remainder = fwd[h, level] - add_up(red_b.at[h, level], rows)
                 solved = mm(remainder.astype(BF16), dinv[level], NN)
@@ -269,7 +286,8 @@
         drain(1 if level == 0 else 2)
         phase += 2
 
-    for h in range(parts):
+    @each
+    def _(h, phase=phase):
         arrived(gath.at[h, 0], h, phase - 1)
         out[0, h] = gath[h, 0].astype(F32)
     drain(0)
@@ -296,8 +314,8 @@
             pltpu.VMEM((parts, pairs, gr, bs), F32),
             pltpu.VMEM((parts, groups * gr, bs), BF16),
             pltpu.VMEM((parts, 2 * pairs, gr, bs), BF16),
-            [[pltpu.VMEM((rep, groups * gr, bs), BF16) for _ in range(parts)]]
-            + [[pltpu.VMEM((rep, groups, gr, bs), BF16) for _ in range(parts)] for _ in range(pairs - 1)],
+            [pltpu.VMEM((parts, rep, groups * gr, bs), BF16)]
+            + [pltpu.VMEM((parts, rep, groups, gr, bs), BF16) for _ in range(pairs - 1)],
             pltpu.VMEM((parts, pairs, groups, gr, bs), BF16),
             pltpu.VMEM((parts, pairs, cols, gr, bs), BF16),
             pltpu.VMEM((parts, cols, groups, gr, bs), BF16),

time: 65.4 us -> 65.1 us (level)
  no operation moved by 1% of the time
where the time goes in v7:
time: 65.1 us; the launch traced here: 64.3 us
  Pallas kernels  63.6 us (98%)
  local copies, waits for them, and re-layouts  0.68 us (1%)
    pallas_call x1, Pallas kernels, per_device(): pl.pallas_call(functools.partial(kernel, (levels, rows, cols, rep, parts,...  63.6 us

profile of v7, /device:TPU:1, one launch (start us, length us, event | category | flops | bytes accessed | tf_op | source)
XLA Modules:
  0.0 64.3 jit_solution(4536162292340172131)
XLA Ops:
  0.0 63.6 %shard_map.46 = f32[3,4,1,16,256]{4,3,2,1,0:T(8,128)S(1)} custom-call(s32[2,2,2]{2,1,0:T(2,128)} %bitcast.11, bf16[3,4,1,16,256]{4,3,2,1,0:T(8,128)(2,1)} %bitcast.10, bf16[3,256,256]{2,1,0:T(8,128)(2,1)} %bitcast.9, bf16[2,2,256,256]{3,2,1,0:T(8,128)(2,1)} %bitcast.8), custom_call_target="tpu_custom_call" | custom-call | tf_op jit(solution)/shard_map/pallas_call | solution.py:303
  63.6 0.7 %copy.7 = f32[3,1,64,256]{3,2,1,0:T(8,128)} copy(f32[3,1,64,256]{3,2,1,0:T(8,128)S(1)} %bitcast.7) | data formatting | bytes 393216

commit v8 on v7

--- a/solution.py
+++ b/solution.py
@@ -68,6 +68,8 @@
     plane = sorted(
         ((dx, dy) for dx in range(nx) for dy in range(ny)), key=lambda d: -2 * ring(d[1], ny) - ring(d[0], nx)
     )
+
+    far_blk = lax.rem((me_r + rows + rows // 2 + cols // 2 - me_c) // cols, rep)
 
     def at_row(k):
         return lax.rem(me_r + k, rows)
@@ -248,7 +250,8 @@
                     total = term if total is None else total + term
                 part_b[h, level, blk] = total.astype(BF16).reshape(groups, gr, bs)
             for g in range(groups - 1, -1, -1):
-                for blk in range(rep):
+                for k in range(rep):
+                    blk = lax.rem(far_blk + k, rep)
                     row = me_c + cols * blk
                     src, dst = part_b.at[h, level, blk, g], red_b.at[h, level, me_r]
                     if g:

time: 65.1 us -> 65.1 us (level)
  no operation moved by 1% of the time
where the time goes in v8:
time: 65.1 us; the launch traced here: 64.3 us
  Pallas kernels  63.6 us (98%)
  local copies, waits for them, and re-layouts  0.68 us (1%)
    pallas_call x1, Pallas kernels, per_device(): pl.pallas_call(functools.partial(kernel, (levels, rows, cols, rep, parts,...  63.6 us

profile of v8, /device:TPU:1, one launch (start us, length us, event | category | flops | bytes accessed | tf_op | source)
XLA Modules:
  0.0 64.3 jit_solution(16080148895647811405)
XLA Ops:
  0.0 63.6 %shard_map.46 = f32[3,4,1,16,256]{4,3,2,1,0:T(8,128)S(1)} custom-call(s32[2,2,2]{2,1,0:T(2,128)} %bitcast.11, bf16[3,4,1,16,256]{4,3,2,1,0:T(8,128)(2,1)} %bitcast.10, bf16[3,256,256]{2,1,0:T(8,128)(2,1)} %bitcast.9, bf16[2,2,256,256]{3,2,1,0:T(8,128)(2,1)} %bitcast.8), custom_call_target="tpu_custom_call" | custom-call | tf_op jit(solution)/shard_map/pallas_call | solution.py:306
  63.6 0.7 %copy.7 = f32[3,1,64,256]{3,2,1,0:T(8,128)} copy(f32[3,1,64,256]{3,2,1,0:T(8,128)S(1)} %bitcast.7) | data formatting | bytes 393216
